TPU v7x, 32 devices: a whole 2x2x4 slice. The times are simulated.
32 devices in a mesh: mol: 2 (over y), row: 16 (over z, x, core).
Axes of the slice: x: 2, y: 2, z: 4, core: 2. Of those that a mesh axis runs over, the one named last changes fastest.
Arguments:
- ia_factor: bfloat16 [768, 3456], P(('mol', 'row')), parts along dimension 0, may hold values from -0.3984375 to 0.3984375
- jb_factor: bfloat16 [221184, 3456], P(('mol', 'row')), parts along dimension 0, may hold values from -0.3984375 to 0.3984375
- eps_occ: float32 [192], P('mol'), parts along dimension 0, may hold values from -2 to -0.3
- eps_vir: float32 [2304], P('mol'), parts along dimension 0, may hold values from 0.2 to 3
Outputs:
- gamma_ia: float32 [768, 3456], P('mol', 'row'), parts along dimension 0
- gamma_jb: bfloat16 [221184, 3456], P(('mol', 'row')), parts along dimension 0
There are 2 independent parts, one for each index of `mol`. A program takes and returns all parts, laid end to end along the dimension named above; each array names one. Nothing has to cross between parts.
All inputs are finite; a program needn't handle non-finite values.
Results may differ from a plain program's by a relative error of at most 0.0047.
Values may be sent and summed in bfloat16 or wider, within the bound.
A program may use at most 256 MiB of HBM per device.

v0:
```python
import jax
import jax.numpy as jnp
from jax import lax
from jax.sharding import PartitionSpec as P

A = 4


os_scale = 1.3


def table_lookup(energies, orbital):
    labels = jnp.arange(energies.shape[0], dtype=jnp.int32)
    return jnp.sum(jnp.where(orbital[:, None] == labels[None, :], energies[None, :], 0.0), axis=1)


def shards(ia_factor, jb_factor, eps_occ, eps_vir):
    vir_count = eps_vir.shape[0]
    jb_count = jb_factor.shape[0]
    global_jb = lax.axis_index("row") * jb_count + jnp.arange(jb_count, dtype=jnp.int32)
    e_jb = table_lookup(eps_vir, global_jb % vir_count) - table_lookup(
        eps_occ, global_jb // vir_count
    )
    slab_eps = eps_vir[:A]
    all_rows = lax.all_gather(ia_factor, "row", axis=0, tiled=True)
    ia_index = jnp.arange(all_rows.shape[0], dtype=jnp.int32)
    e_ia = table_lookup(slab_eps, ia_index % A) - table_lookup(eps_occ, ia_index // A)
    coulomb = lax.dot_general(
        all_rows, jb_factor, (((1,), (1,)), ((), ())), preferred_element_type=jnp.float32
    )
    amplitude = (-os_scale * coulomb / (e_ia[:, None] + e_jb[None, :])).astype(jnp.bfloat16)
    gamma_jb = lax.dot_general(
        amplitude, all_rows, (((0,), (0,)), ((), ())), preferred_element_type=jnp.float32
    ).astype(jnp.bfloat16)
    summed_rows = lax.psum_scatter(
        jnp.dot(amplitude, jb_factor, preferred_element_type=jnp.float32),
        "row",
        scatter_dimension=0,
        tiled=True,
    )
    gamma_ia = lax.all_to_all(summed_rows, "row", split_axis=1, concat_axis=0, tiled=True)
    return (gamma_ia, gamma_jb)


def solution(mesh):
    placed = (P(("mol", "row"), None), P(("mol", "row"), None), P("mol"), P("mol"))
    return jax.shard_map(
        shards,
        mesh=mesh,
        in_specs=placed,
        out_specs=(P("mol", "row"), P(("mol", "row"), None)),
        check_vma=False,
    )
```

profile of v0, /device:TPU:0, one launch (start us, length us, event | category | flops | bytes accessed | tf_op | source)
XLA Modules:
  0.0 244.2 jit_solution(4292790459668209135)
XLA Ops:
  7.2 0.0 all-gather.2.cloned.1.call-start
  7.2 0.7 all-gather.2.cloned.1.call-update
  7.9 0.0 reduce-scatter.4.cloned.1.call-start
  7.9 0.7 slice.3
  8.6 0.1 select_reduce_fusion.3
  8.7 0.7 select_reduce_fusion.2
  9.5 1.1 select_reduce_fusion.1
  10.7 7.3 %select_reduce_fusion = f32[6912]{0:T(1024)S(1)} fusion(f32[1152]{0:T(1024)} %param.7, s32[6912]{0:T(1024)S(1)} %get-tuple-element.9), kind=kLoop, calls=%fused_computation.1 | loop fusion | flops 23880960 | bytes 59904 | tf_op jit(solution)/shard_map/reduce_sum | solution.py:14
  17.9 38.2 %all-gather.2.cloned.1.call-done = bf16[384,3456]{1,0:T(8,128)(2,1)} async-done(((bf16[24,3456]{1,0:T(8,128)(2,1)}), bf16[384,3456]{1,0:T(8,128)(2,1)}) %all-gather.2.cloned.1.call-update) | async-done | bytes 2654224 | tf_op jit(solution)/shard_map/all_gather | solution.py:25
  56.2 27.7 %fusion.19 = f32[384,6912]{1,0:T(8,128)} fusion(bf16[384,3456]{1,0:T(8,128)(2,1)} %all-gather.2.cloned.1.call-done, bf16[6912,3456]{1,0:T(8,128)(2,1)} %param.5), kind=kOutput, calls=%fused_computation.38 | convolution fusion | flops 18345885696 | bytes 61046784 | tf_op jit(solution)/shard_map/dot_general | solution.py:28
  83.9 0.0 copy-start
  83.9 31.8 %fusion = f32[384,3456]{1,0:T(8,128)} fusion(bf16[6912,3456]{1,0:T(8,128)(2,1)} %param.5, f32[384,6912]{1,0:T(8,128)} %fusion.19, f32[6912]{0:T(1024)S(1)} %sub.29, f32[384]{0:T(512)S(1)} %sub.27), kind=kOutput, calls=%fused_computation.4 | convolution fusion | flops 18356502528 | bytes 63730176 | tf_op jit(solution)/shard_map/dot_general | solution.py:36
  115.7 0.0 reduce-scatter.4.cloned.1.call-update
  115.7 78.4 %reduce-scatter.4.cloned.1.call-done = f32[24,3456]{1,0:T(8,128)} async-done(((f32[384,3456]{1,0:T(8,128)}), f32[24,3456]{1,0:T(8,128)}) %reduce-scatter.4.cloned.1.call-update) | async-done | bytes 331792
  194.1 1.5 all_to_all.14
  195.6 1.0 copy.11
  196.6 3.8 %all-to-all-start = ((f32[24,16,216]{2,0,1:T(8,128)}), f32[24,16,216]{2,0,1:T(8,128)S(1)}, u32[]{:S(2)}, u32[]{:S(2)}) async-start(f32[24,16,216]{2,0,1:T(8,128)} %copy.11), calls=%async_computation | async-start | bytes 786432 | tf_op jit(solution)/shard_map/all_to_all | solution.py:41
  200.4 0.0 copy-done
  200.4 36.0 %convolution_convert_fusion = bf16[6912,3456]{1,0:T(8,128)(2,1)} fusion(bf16[384,3456]{1,0:T(8,128)(2,1)S(1)} %copy-done, f32[384,6912]{1,0:T(8,128)} %fusion.19, f32[6912]{0:T(1024)S(1)} %sub.29, f32[384]{0:T(512)S(1)} %sub.27), kind=kOutput, calls=%fused_computation | convolution fusion | flops 18380390400 | bytes 61075968 | tf_op jit(solution)/shard_map/dot_general | solution.py:32
  236.4 0.0 all-to-all-done
  236.4 0.9 copy.12
  (5 shorter events, 0.1 us)
Async XLA Ops:
  7.2 49.0 %all-gather.2.cloned.1.call-start = ((), (), s32[]{:S(2)}) async-start(), calls=%async_computation.2 | async-start | bytes 2820096 | tf_op jit(solution)/shard_map/all_gather | solution.py:25
  7.9 186.2 %reduce-scatter.4.cloned.1.call-start = ((), (), s32[]{:S(2)}) async-start(), calls=%async_computation.3 | async-start | bytes 5640192
  83.9 116.6 %copy-start = (bf16[384,3456]{1,0:T(8,128)(2,1)S(1)}, bf16[384,3456]{1,0:T(8,128)(2,1)}, u32[]{:S(2)}) copy-start(bf16[384,3456]{1,0:T(8,128)(2,1)} %all-gather.2.cloned.1.call-done) | copy-start | bytes 7962628
  196.6 39.8 %all-to-all-start = ((f32[24,16,216]{2,0,1:T(8,128)}), f32[24,16,216]{2,0,1:T(8,128)S(1)}, u32[]{:S(2)}, u32[]{:S(2)}) async-start(f32[24,16,216]{2,0,1:T(8,128)} %copy.11), calls=%async_computation | async-start | bytes 786432 | tf_op jit(solution)/shard_map/all_to_all | solution.py:41
Sparse Core Ops, SparseCore 0:
  10.1 45.9 all-gather.1
  115.9 78.2 reduce-scatter.3
where the time goes:
time: 245 us; the launch traced here: 244 us
  waiting for transfers between devices  117 us (48%)
  matrix products  95.5 us (39%)
  between operations  14.1 us (6%)
  other arithmetic  9.28 us (4%)
  local copies, waits for them, and re-layouts  4.09 us (2%)
  starting transfers between devices  3.86 us (2%)
    unnamed x3, waiting for transfers between devices  79.1 us
    all_gather x1, waiting for transfers between devices, shards(): all_rows = lax.all_gather(ia_factor, 'row', axis=0, tiled=True)  38.2 us
    dot_general x1, matrix products, shards(): lax.dot_general(amplitude, all_rows, (((0,), (0,)), ((), ())), preferred_...  36 us
    dot_general x1, matrix products, shards(): jnp.dot(amplitude, jb_factor, preferred_element_type=jnp.float32)  31.8 us
    dot_general x1, matrix products, shards(): lax.dot_general(all_rows, jb_factor, (((1,), (1,)), ((), ())), preferred_...  27.7 us
    reduce_sum x4, other arithmetic, table_lookup(): jnp.sum(jnp.where(orbital[:, None] == labels[None, :], energies[None, :],...  9.22 us
  transfers between devices with their start and end apart: 3, of which 2 were waited for; matrix products, arithmetic and copies ran while one was open for 19% of the time, Pallas kernels for 0%

commit v1 on v0

v1 whole, which is shorter than its diff:
```python
import functools

import jax
import jax.numpy as jnp
from jax import lax
from jax.experimental import pallas as pl
from jax.experimental.pallas import tpu as pltpu
from jax.sharding import PartitionSpec as P

A = 4
os_scale = 1.3
MESH = pl.DeviceIdType.MESH


def bit_orders(n):
    bits = n.bit_length() - 1
    first = [b for b in (1,) if b < bits]
    far = list(range(bits - 1, 1, -1))
    near = [0] if bits else []
    return first + far + near, far + first + near


def subsets(bits):
    out = [0]
    for b in bits:
        out = out + [s | (1 << b) for s in out]
    return out


def flip(me, mask, bits):
    for b in range(bits):
        if mask >> b & 1:
            me = me + (1 << b) * (1 - 2 * ((me // (1 << b)) % 2))
    return me


def enter(me, bits):
    barrier = pltpu.get_barrier_semaphore()
    for b in range(bits):
        pl.semaphore_signal(
            barrier, inc=1, device_id={"row": flip(me, 1 << b, bits)}, device_id_type=MESH
        )
    pl.semaphore_wait(barrier, bits)


def gather_kernel(n, spans, x_ref, out_ref, own_sem, send_sem, recv_sem):
    bits = n.bit_length() - 1
    me = lax.axis_index("row")
    own = pltpu.make_async_copy(x_ref, out_ref.at[me], own_sem)
    own.start()
    enter(me, bits)

    def copy(h, m, b):
        start, size = spans[h]
        s = m ^ (1 << b)
        block = flip(me, s, bits)
        src = x_ref if s == 0 else out_ref.at[block]
        return pltpu.make_async_remote_copy(
            src_ref=src.at[:, pl.ds(start, size)],
            dst_ref=out_ref.at[block, :, pl.ds(start, size)],
            send_sem=send_sem.at[h, m],
            recv_sem=recv_sem.at[h, m],
            device_id={"row": flip(me, 1 << b, bits)},
            device_id_type=MESH,
        )

    orders = bit_orders(n)
    started = {}
    for p in range(bits):
        for h in range(2):
            b = orders[h][p]
            for s in subsets(orders[h][:p]):
                if s:
                    started[h, s].wait_recv()
                m = s | (1 << b)
                started[h, m] = Once(copy(h, m, b))
                started[h, m].start()
    for c in started.values():
        c.wait_recv()
        c.wait_send()
    own.wait()


class Once:
    def __init__(self, copy):
        self.copy, self.got = copy, False

    def start(self):
        self.copy.start()

    def wait_send(self):
        self.copy.wait_send()

    def wait_recv(self):
        if not self.got:
            self.got = True
            self.copy.wait_recv()


def gather(ia, n):
    r, c = ia.shape
    half = (c // 128 + 1) // 2 * 128
    spans = ((0, half), (half, c - half))
    return pl.pallas_call(
        functools.partial(gather_kernel, n, spans),
        out_shape=jax.ShapeDtypeStruct((n, r, c), ia.dtype),
        in_specs=[pl.BlockSpec(memory_space=pl.ANY)],
        out_specs=pl.BlockSpec(memory_space=pl.ANY),
        scratch_shapes=[
            pltpu.SemaphoreType.DMA,
            pltpu.SemaphoreType.DMA((2, n)),
            pltpu.SemaphoreType.DMA((2, n)),
        ],
        compiler_params=pltpu.CompilerParams(collective_id=0, has_side_effects=True),
        name="gather_ia",
    )(ia)


def dense_kernel(n, ia_ref, jb_ref, eia_ref, ejb_ref, gjb_ref, part_ref, acc):
    step = pl.program_id(0)

    @pl.when(step == 0)
    def _():
        acc[...] = jnp.zeros_like(acc)

    coulomb = lax.dot_general(
        ia_ref[...], jb_ref[...], (((1,), (1,)), ((), ())), preferred_element_type=jnp.float32
    )
    denom = eia_ref[...] + ejb_ref[0]
    amp = (-os_scale * coulomb / denom).astype(jnp.bfloat16)
    gjb_ref[...] = lax.dot_general(
        amp, ia_ref[...], (((0,), (0,)), ((), ())), preferred_element_type=jnp.float32
    ).astype(jnp.bfloat16)
    acc[...] += jnp.dot(amp, jb_ref[...], preferred_element_type=jnp.float32)

    @pl.when(step == pl.num_programs(0) - 1)
    def _():
        w = part_ref.shape[2]
        for d in range(n):
            part_ref[d] = acc[:, d * w : (d + 1) * w]


def tile_of(rows):
    for t in (256, 768, 384, 288, 128):
        if rows % t == 0:
            return t
    return rows


def dense(ia, jb, e_ia, e_jb, n):
    m, c = ia.shape
    rows = jb.shape[0]
    t = tile_of(rows)
    return pl.pallas_call(
        functools.partial(dense_kernel, n),
        grid=(rows // t,),
        out_shape=(
            jax.ShapeDtypeStruct((rows, c), jnp.bfloat16),
            jax.ShapeDtypeStruct((n, m, c // n), jnp.float32),
        ),
        in_specs=[
            pl.BlockSpec((m, c), lambda i: (0, 0)),
            pl.BlockSpec((t, c), lambda i: (i, 0)),
            pl.BlockSpec((m, 1), lambda i: (0, 0)),
            pl.BlockSpec((1, 1, t), lambda i: (i, 0, 0)),
        ],
        out_specs=(
            pl.BlockSpec((t, c), lambda i: (i, 0)),
            pl.BlockSpec((n, m, c // n), lambda i: (0, 0, 0)),
        ),
        scratch_shapes=[pltpu.VMEM((m, c), jnp.float32)],
        compiler_params=pltpu.CompilerParams(
            dimension_semantics=("arbitrary",), vmem_limit_bytes=60 * 2**20
        ),
        cost_estimate=pl.CostEstimate(
            flops=6 * m * rows * c, bytes_accessed=4 * rows * c, transcendentals=0
        ),
        name="densities",
    )(ia, jb, e_ia, e_jb.reshape(rows // t, 1, t))


def reduce_kernel(n, part_hbm, out_ref, part_ref, stage, recv, load_sem, send_sem, recv_sem):
    bits = n.bit_length() - 1
    me = lax.axis_index("row")
    half = part_ref.shape[1] // 2
    load = pltpu.make_async_copy(part_hbm, part_ref, load_sem)
    load.start()
    enter(me, bits)
    load.wait()
    orders = [order[::-1] for order in bit_orders(n)]
    copies = []
    pending = {}
    for p in range(bits):
        for h in range(2):
            rows = pl.ds(h * half, half)
            if p:
                for s, m in pending[h]:
                    keep = flip(me, s, bits)
                    part_ref[keep, rows] = part_ref[keep, rows] + recv[h, m].astype(jnp.float32)
            b = orders[h][p]
            sent = []
            for s in subsets(orders[h][p + 1 :]):
                m = s | (1 << b)
                stage[h, m] = part_ref[flip(me, m, bits), rows].astype(jnp.bfloat16)
                c = pltpu.make_async_remote_copy(
                    src_ref=stage.at[h, m],
                    dst_ref=recv.at[h, m],
                    send_sem=send_sem.at[h, m],
                    recv_sem=recv_sem.at[h, m],
                    device_id={"row": flip(me, 1 << b, bits)},
                    device_id_type=MESH,
                )
                c.start()
                copies.append(c)
                sent.append((s, m, c))
            pending[h] = [Pair(s, m, c) for s, m, c in sent]
    for h in range(2):
        rows = pl.ds(h * half, half)
        for s, m in pending[h]:
            out_ref[rows] = part_ref[me, rows] + recv[h, m].astype(jnp.float32)
    for c in copies:
        c.wait_send()


class Pair:
    def __init__(self, s, m, copy):
        self.s, self.m, self.copy = s, m, copy

    def __iter__(self):
        self.copy.wait_recv()
        return iter((self.s, self.m))


def reduce_scatter(part, n):
    _, m, w = part.shape
    return pl.pallas_call(
        functools.partial(reduce_kernel, n),
        out_shape=jax.ShapeDtypeStruct((m, w), jnp.float32),
        in_specs=[pl.BlockSpec(memory_space=pl.ANY)],
        out_specs=pl.BlockSpec(memory_space=pltpu.VMEM),
        scratch_shapes=[
            pltpu.VMEM((n, m, w), jnp.float32),
            pltpu.VMEM((2, n, m // 2, w), jnp.bfloat16),
            pltpu.VMEM((2, n, m // 2, w), jnp.bfloat16),
            pltpu.SemaphoreType.DMA,
            pltpu.SemaphoreType.DMA((2, n)),
            pltpu.SemaphoreType.DMA((2, n)),
        ],
        compiler_params=pltpu.CompilerParams(
            collective_id=1, has_side_effects=True, vmem_limit_bytes=60 * 2**20
        ),
        name="reduce_gamma",
    )(part)


def shards(n, ia_factor, jb_factor, eps_occ, eps_vir):
    jb_count = jb_factor.shape[0]
    pairs = (eps_vir[None, :] - eps_occ[:, None]).reshape(-1)
    e_jb = lax.dynamic_slice_in_dim(pairs, lax.axis_index("row") * jb_count, jb_count)
    e_ia = (eps_vir[:A][None, :] - eps_occ[:, None]).reshape(-1, 1)
    all_rows = gather(ia_factor, n).reshape(-1, ia_factor.shape[1])
    gamma_jb, part = dense(all_rows, jb_factor, e_ia, e_jb, n)
    return (reduce_scatter(part, n), gamma_jb)


def solution(mesh):
    placed = (P(("mol", "row"), None), P(("mol", "row"), None), P("mol"), P("mol"))
    return jax.shard_map(
        functools.partial(shards, mesh.shape["row"]),
        mesh=mesh,
        in_specs=placed,
        out_specs=(P("mol", "row"), P(("mol", "row"), None)),
        check_vma=False,
    )
```

time: 245 us -> 188 us (0.77)
  Pallas kernels: 0 us -> 181 us
  waiting for transfers between devices: 117 us -> 0 us
  matrix products: 95.5 us -> 0 us
  between operations: 14.1 us -> 0.68 us
  other arithmetic: 9.28 us -> 1.53 us
  starting transfers between devices: 3.86 us -> 0 us
    pallas_call x0 -> x3, Pallas kernels: none -> 181 us  [the longest x1 121 us: dense(): pl.pallas_call(functools.partial(dense_kernel, n), grid=(rows // t,), out...]
    dot_general x3 -> x0, matrix products: 95.5 us -> none  [the longest x1 36 us: shards(): lax.dot_general(amplitude, all_rows, (((0,), (0,)), ((), ())), preferred_...]
    unnamed x3 -> x0, waiting for transfers between devices: 79.1 us -> none
    all_gather x1 -> x0, waiting for transfers between devices: 38.2 us -> none  [shards(): all_rows = lax.all_gather(ia_factor, 'row', axis=0, tiled=True)]
    reduce_sum x4 -> x0, other arithmetic: 9.22 us -> none  [table_lookup(): jnp.sum(jnp.where(orbital[:, None] == labels[None, :], energies[None, :],...]
    all_to_all x1 -> x0, starting transfers between devices: 3.78 us -> none  [shards(): lax.all_to_all(summed_rows, 'row', split_axis=1, concat_axis=0, tiled=True)]
    all_to_all x2 -> x0, local copies, waits for them, and re-layouts: 2.51 us -> none  [shards(): lax.all_to_all(summed_rows, 'row', split_axis=1, concat_axis=0, tiled=True)]
  transfers between devices with their start and end apart: 3 -> 0, of which waited for: 2 -> 0; matrix products, arithmetic and copies ran while one was open for 19% -> 0% of each run, Pallas kernels for 0% -> 0%
where the time goes in v1:
time: 188 us; the launch traced here: 187 us
  Pallas kernels  181 us (96%)
  local copies, waits for them, and re-layouts  4.12 us (2%)
    pallas_call x1, Pallas kernels, dense(): pl.pallas_call(functools.partial(dense_kernel, n), grid=(rows // t,), out...  121 us
    pallas_call x1, Pallas kernels, reduce_scatter(): pl.pallas_call(functools.partial(reduce_kernel, n), out_shape=jax.ShapeDt...  32.4 us
    pallas_call x1, Pallas kernels, gather(): pl.pallas_call(functools.partial(gather_kernel, n, spans), out_shape=jax....  28.1 us

profile of v1, /device:TPU:0, one launch (start us, length us, event | category | flops | bytes accessed | tf_op | source)
XLA Modules:
  0.0 187.5 jit_solution(11781036707978371579)
XLA Ops:
  0.6 0.7 slice.3
  1.3 0.7 broadcast_subtract_fusion.1
  2.1 0.8 sub.48.eia_ref
  2.8 0.8 broadcast_subtract_fusion
  3.7 0.1 dynamic_slice.3
  3.8 0.6 reshape.41.ejb_ref
  4.4 28.1 %gather_ia.1 = bf16[16,24,3456]{2,1,0:T(8,128)(2,1)} custom-call(bf16[24,3456]{1,0:T(8,128)(2,1)} %x_ref.1), custom_call_target="tpu_custom_call" | custom-call | tf_op jit(solution)/shard_map/gather_ia/pallas_call | solution.py:104
  32.6 120.7 %densities.1 = (bf16[6912,3456]{1,0:T(8,128)(2,1)}, f32[16,384,216]{2,1,0:T(8,128)}) custom-call(bf16[384,3456]{1,0:T(8,128)(2,1)} %bitcast.1, bf16[6912,3456]{1,0:T(8,128)(2,1)} %jb_ref.1, f32[384,1]{1,0:T(8,128)} %sub.48.eia_ref, f32[27,1,256]{2,1,0:T(1,128)} %reshape.41.ejb_ref), custom_call_target="tpu_custom_call" | custom-call | flops 55037657088 | bytes 95551488 | tf_op jit(solution)/shard_map/densities/pallas_call | solution.py:154
  153.2 32.4 %reduce_gamma.1 = f32[384,216]{1,0:T(8,128)} custom-call(f32[16,384,216]{2,1,0:T(8,128)} %get-tuple-element.4.part_hbm), custom_call_target="tpu_custom_call" | custom-call | tf_op jit(solution)/shard_map/reduce_gamma/pallas_call | solution.py:236
  185.6 1.9 %copy.8 = f32[384,216]{0,1:T(8,128)} copy(f32[384,216]{1,0:T(8,128)} %reduce_gamma.1) | data formatting | bytes 663552
  (1 shorter events, 0.0 us)

commit v2 on v1

--- a/solution.py
+++ b/solution.py
@@ -124,14 +124,15 @@
         acc[...] = jnp.zeros_like(acc)
 
     coulomb = lax.dot_general(
-        ia_ref[...], jb_ref[...], (((1,), (1,)), ((), ())), preferred_element_type=jnp.float32
+        jb_ref[...], ia_ref[...], (((1,), (1,)), ((), ())), preferred_element_type=jnp.float32
     )
-    denom = eia_ref[...] + ejb_ref[0]
+    e_jb = jnp.broadcast_to(ejb_ref[0], (128, ejb_ref.shape[2])).T
+    denom = eia_ref[...] + e_jb[:, :1]
     amp = (-os_scale * coulomb / denom).astype(jnp.bfloat16)
-    gjb_ref[...] = lax.dot_general(
-        amp, ia_ref[...], (((0,), (0,)), ((), ())), preferred_element_type=jnp.float32
+    gjb_ref[...] = jnp.dot(
+        amp, ia_ref[...], preferred_element_type=jnp.float32
     ).astype(jnp.bfloat16)
-    acc[...] += jnp.dot(amp, jb_ref[...], preferred_element_type=jnp.float32)
+    acc[...] += jnp.dot(amp.T, jb_ref[...], preferred_element_type=jnp.float32)
 
     @pl.when(step == pl.num_programs(0) - 1)
     def _():
@@ -141,7 +142,7 @@
 
 
 def tile_of(rows):
-    for t in (256, 768, 384, 288, 128):
+    for t in (768, 256, 384, 288, 128):
         if rows % t == 0:
             return t
     return rows
@@ -159,14 +160,14 @@
             jax.ShapeDtypeStruct((n, m, c // n), jnp.float32),
         ),
         in_specs=[
-            pl.BlockSpec((m, c), lambda i: (0, 0)),
+            pl.BlockSpec((m, c), lambda i: (0, 0), pipeline_mode=pl.Buffered(1)),
             pl.BlockSpec((t, c), lambda i: (i, 0)),
-            pl.BlockSpec((m, 1), lambda i: (0, 0)),
+            pl.BlockSpec((1, m), lambda i: (0, 0)),
             pl.BlockSpec((1, 1, t), lambda i: (i, 0, 0)),
         ],
         out_specs=(
             pl.BlockSpec((t, c), lambda i: (i, 0)),
-            pl.BlockSpec((n, m, c // n), lambda i: (0, 0, 0)),
+            pl.BlockSpec((n, m, c // n), lambda i: (0, 0, 0), pipeline_mode=pl.Buffered(1)),
         ),
         scratch_shapes=[pltpu.VMEM((m, c), jnp.float32)],
         compiler_params=pltpu.CompilerParams(
@@ -257,7 +258,7 @@
     jb_count = jb_factor.shape[0]
     pairs = (eps_vir[None, :] - eps_occ[:, None]).reshape(-1)
     e_jb = lax.dynamic_slice_in_dim(pairs, lax.axis_index("row") * jb_count, jb_count)
-    e_ia = (eps_vir[:A][None, :] - eps_occ[:, None]).reshape(-1, 1)
+    e_ia = (eps_vir[:A][None, :] - eps_occ[:, None]).reshape(1, -1)
     all_rows = gather(ia_factor, n).reshape(-1, ia_factor.shape[1])
     gamma_jb, part = dense(all_rows, jb_factor, e_ia, e_jb, n)
     return (reduce_scatter(part, n), gamma_jb)

time: 188 us -> 148 us (0.79)
  Pallas kernels: 181 us -> 142 us
    pallas_call x1, Pallas kernels: 121 us -> 82.2 us  [dense(): pl.pallas_call(functools.partial(dense_kernel, n), grid=(rows // t,), out...]
where the time goes in v2:
time: 148 us
  Pallas kernels  142 us (96%)
  local copies, waits for them, and re-layouts  4.01 us (3%)
  other arithmetic  1.53 us (1%)
    pallas_call x1, Pallas kernels, dense(): pl.pallas_call(functools.partial(dense_kernel, n), grid=(rows // t,), out...  82.2 us
    pallas_call x1, Pallas kernels, reduce_scatter(): pl.pallas_call(functools.partial(reduce_kernel, n), out_shape=jax.ShapeDt...  31.3 us
    pallas_call x1, Pallas kernels, gather(): pl.pallas_call(functools.partial(gather_kernel, n, spans), out_shape=jax....  28.1 us

profile of v2, /device:TPU:0, one launch (start us, length us, event | category | flops | bytes accessed | tf_op | source)
XLA Modules:
  0.0 147.8 jit_solution(3637765174588347614)
XLA Ops:
  0.6 0.7 slice.3
  1.3 0.7 broadcast_subtract_fusion.1
  2.1 0.7 sub.43.eia_ref
  2.7 0.8 broadcast_subtract_fusion
  3.6 0.1 dynamic_slice.3
  3.7 0.6 reshape.41.ejb_ref
  4.3 28.1 %gather_ia.1 = bf16[16,24,3456]{2,1,0:T(8,128)(2,1)} custom-call(bf16[24,3456]{1,0:T(8,128)(2,1)} %x_ref.1), custom_call_target="tpu_custom_call" | custom-call | tf_op jit(solution)/shard_map/gather_ia/pallas_call | solution.py:104
  32.5 82.2 %densities.1 = (bf16[6912,3456]{1,0:T(8,128)(2,1)}, f32[16,384,216]{2,1,0:T(8,128)}) custom-call(bf16[384,3456]{1,0:T(8,128)(2,1)} %bitcast.1, bf16[6912,3456]{1,0:T(8,128)(2,1)} %jb_ref.1, f32[1,384]{1,0:T(1,128)} %sub.43.eia_ref, f32[9,1,768]{2,1,0:T(1,128)} %reshape.41.ejb_ref), custom_call_target="tpu_custom_call" | custom-call | flops 55037657088 | bytes 95551488 | tf_op jit(solution)/shard_map/densities/pallas_call | solution.py:155
  114.7 31.3 %reduce_gamma.1 = f32[384,216]{1,0:T(8,128)} custom-call(f32[16,384,216]{2,1,0:T(8,128)} %get-tuple-element.4.part_hbm), custom_call_target="tpu_custom_call" | custom-call | tf_op jit(solution)/shard_map/reduce_gamma/pallas_call | solution.py:237
  146.0 1.9 %copy.7 = f32[384,216]{0,1:T(8,128)} copy(f32[384,216]{1,0:T(8,128)} %reduce_gamma.1) | data formatting | bytes 663552
  (1 shorter events, 0.0 us)
